TPU v7x, 32 devices: a whole 2x2x4 slice. The times are simulated.
32 devices in a mesh: seq: 8 (over y, x, core), tp: 4 (over z).
Axes of the slice: x: 2, y: 2, z: 4, core: 2. Of those that a mesh axis runs over, the one named last changes fastest.
Arguments:
- tokens: bfloat16 [256, 8, 1152], P(None, 'seq'), may hold values from -6 to 6
- grad_out: bfloat16 [256, 8, 1152], P('seq'), may hold values from -6 to 6
- qkv_weight: bfloat16 [2, 1152, 3, 1152], P(None, None, None, 'tp'), may hold values from -1 to 1
- out_weight: bfloat16 [2, 1152, 1152], P(None, 'tp'), may hold values from -0.1875 to 0.1875
- mod_shift: float32 [2, 1152], replicated, may hold values from -3 to 3
- mod_scale: float32 [2, 1152], replicated, may hold values from -1.8 to 1.8
- mod_gate: float32 [2, 1152], replicated, may hold values from 0.5 to 1.5
Outputs:
- result: bfloat16 [256, 8, 1152], P('seq')
- grad_in: bfloat16 [256, 8, 1152], P(None, 'seq')
All inputs are finite; a program needn't handle non-finite values.
Results may differ from a plain program's by a relative error of at most 0.035.
Values may be sent and summed in bfloat16 or wider, within the bound.
A program may use at most 64 MiB of HBM per device.

v0:
```python
import math

import jax
import jax.numpy as jnp
from jax import lax
from jax.sharding import PartitionSpec as P

HEAD_DIM = 72


SPATIAL = ("pfhd,qfhd->fhpq", "fhpq,qfhd->pfhd", "fhpq,pfhd->qfhd")
TEMPORAL = ("pfhd,pghd->phfg", "phfg,pghd->pfhd", "phfg,pfhd->pghd")


def normalize(tokens, shift_row, scale_row):
    widened = tokens.astype(jnp.float32)
    center = widened - jnp.mean(widened, axis=-1, keepdims=True)
    inv_std = lax.rsqrt(jnp.mean(center * center, axis=-1, keepdims=True) + 1e-06)
    normed = center * inv_std
    modded = (normed * (1.0 + scale_row) + shift_row).astype(jnp.bfloat16)
    return (modded, normed, inv_std)


def attend(tokens, qkv_weights, shift_row, scale_row, layout_forms):
    modded, normed, inv_std = normalize(tokens, shift_row, scale_row)
    projected = jnp.einsum(
        "abd,dce->abce", modded, qkv_weights, preferred_element_type=jnp.float32
    ).astype(jnp.bfloat16)
    heads_here = qkv_weights.shape[2] // HEAD_DIM
    projected = projected.reshape(tokens.shape[0], tokens.shape[1], 3, heads_here, HEAD_DIM)
    queries, key_heads, value_heads = (projected[:, :, 0], projected[:, :, 1], projected[:, :, 2])
    scores = jnp.einsum(
        layout_forms[0], queries, key_heads, preferred_element_type=jnp.float32
    ) / math.sqrt(HEAD_DIM)
    probs_high = jax.nn.softmax(scores, axis=-1)
    probs_low = probs_high.astype(jnp.bfloat16)
    attended = jnp.einsum(
        layout_forms[1], probs_low, value_heads, preferred_element_type=jnp.float32
    ).astype(jnp.bfloat16)
    attended = attended.reshape(tokens.shape[0], tokens.shape[1], -1)
    return (attended, (normed, inv_std, queries, key_heads, value_heads, probs_high, probs_low))


def attend_back(grad, cache, out_matrix, gate_row, layout_forms):
    normed, inv_std, queries, key_heads, value_heads, probs_high, probs_low = cache
    grad_proj = (gate_row * grad.astype(jnp.float32)).astype(jnp.bfloat16)
    grad_attn = jnp.einsum(
        "abd,ed->abe", grad_proj, out_matrix, preferred_element_type=jnp.float32
    ).astype(jnp.bfloat16)
    grad_attn = grad_attn.reshape(queries.shape)
    grad_probs = jnp.einsum(
        layout_forms[0], grad_attn, value_heads, preferred_element_type=jnp.float32
    )
    grad_scores = (
        probs_high
        * (grad_probs - jnp.sum(probs_high * grad_probs, axis=-1, keepdims=True))
        / math.sqrt(HEAD_DIM)
    ).astype(jnp.bfloat16)
    grad_query = jnp.einsum(
        layout_forms[1], grad_scores, key_heads, preferred_element_type=jnp.float32
    ).astype(jnp.bfloat16)
    grad_keys = jnp.einsum(
        layout_forms[2], grad_scores, queries, preferred_element_type=jnp.float32
    ).astype(jnp.bfloat16)
    grad_values = jnp.einsum(
        layout_forms[2], probs_low, grad_attn, preferred_element_type=jnp.float32
    ).astype(jnp.bfloat16)
    stacked = jnp.stack([grad_query, grad_keys, grad_values], axis=2)
    return stacked.reshape(queries.shape[0], queries.shape[1], 3, -1)


def norm_back(grad_mod, normed, inv_std, scale_row):
    grad_norm = grad_mod * (1.0 + scale_row)
    return inv_std * (
        grad_norm
        - jnp.mean(grad_norm, axis=-1, keepdims=True)
        - normed * jnp.mean(grad_norm * normed, axis=-1, keepdims=True)
    )


def head_total(partial_value):
    return lax.psum(partial_value.astype(jnp.bfloat16), "tp").astype(jnp.float32)


def to_patches(frame_rows):
    return lax.all_to_all(frame_rows, "seq", split_axis=0, concat_axis=1, tiled=True)


def to_frames(patch_rows):
    return lax.all_to_all(patch_rows, "seq", split_axis=1, concat_axis=0, tiled=True)


def per_device(tokens, grad_out, qkv_weight, out_weight, mod_shift, mod_scale, mod_gate):
    attended, cache_s = attend(tokens, qkv_weight[0], mod_shift[0], mod_scale[0], SPATIAL)
    partial_value = jnp.einsum(
        "abe,ed->abd", attended, out_weight[0], preferred_element_type=jnp.float32
    )
    middle = (tokens.astype(jnp.float32) + mod_gate[0] * head_total(partial_value)).astype(
        jnp.bfloat16
    )
    mid_patch = to_patches(middle)
    attended_t, cache_t = attend(mid_patch, qkv_weight[1], mod_shift[1], mod_scale[1], TEMPORAL)
    partial_t = jnp.einsum(
        "abe,ed->abd", attended_t, out_weight[1], preferred_element_type=jnp.float32
    )
    result = (mid_patch.astype(jnp.float32) + mod_gate[1] * head_total(partial_t)).astype(
        jnp.bfloat16
    )
    stacked_t = attend_back(grad_out, cache_t, out_weight[1], mod_gate[1], TEMPORAL)
    normed_t, inv_std_t = (cache_t[0], cache_t[1])
    grad_mod = head_total(
        jnp.einsum("abce,dce->abd", stacked_t, qkv_weight[1], preferred_element_type=jnp.float32)
    )
    grad_patch = (
        grad_out.astype(jnp.float32) + norm_back(grad_mod, normed_t, inv_std_t, mod_scale[1])
    ).astype(jnp.bfloat16)
    grad_mid = to_frames(grad_patch)
    stacked_s = attend_back(grad_mid, cache_s, out_weight[0], mod_gate[0], SPATIAL)
    grad_mod_s = head_total(
        jnp.einsum("abce,dce->abd", stacked_s, qkv_weight[0], preferred_element_type=jnp.float32)
    )
    grad_in = (
        grad_mid.astype(jnp.float32) + norm_back(grad_mod_s, cache_s[0], cache_s[1], mod_scale[0])
    ).astype(jnp.bfloat16)
    return (result, grad_in)


def solution(mesh):
    in_specs = (
        P(None, "seq", None),
        P("seq", None, None),
        P(None, None, None, "tp"),
        P(None, "tp", None),
        P(),
        P(),
        P(),
    )
    out_specs = (P("seq", None, None), P(None, "seq", None))
    return jax.shard_map(
        per_device, mesh=mesh, in_specs=in_specs, out_specs=out_specs, check_vma=False
    )
```

profile of v0, /device:TPU:0, one launch (start us, length us, event | category | flops | bytes accessed | tf_op | source)
XLA Modules:
  0.0 234.7 jit_solution(498488391659009107)
XLA Ops:
  7.2 0.0 all-reduce.5.cloned.1.call-start
  7.2 1.3 convert_reduce_fusion
  8.5 1.4 fusion.48
  9.9 0.1 slice_reduce_fusion
  10.0 2.4 %fusion.33 = bf16[256,3,288]{0,2,1:T(8,128)(2,1)S(1)} fusion(bf16[2,1152,3,288]{1,3,2,0:T(8,128)(2,1)} %param.9, bf16[256,1,1152]{2,0,1:T(8,128)(2,1)S(1)} %copy-done, f32[1152]{0:T(1024)S(1)} %get-tuple-element.11, f32[1152]{0:T(1024)S(1)} %get-tuple-element.21, f32[256]{0:T(256)S(1)} %add_rsqrt_fusion.1, f32[256]{0:T(256)S(1)} %broadcast_multiply_fusion.5), kind=kOutput, calls=%fused_computation.41 | convolution fusion | flops 511598592 | bytes 3034112 | tf_op jit(solution)/shard_map/abd,dce->abce/dot_general | solution.py:26
  12.5 1.5 fusion.133
  14.0 0.7 convolution_convert_fusion.10
  14.8 0.6 copy-done.1
  15.3 1.3 fusion.6
  16.7 0.0 all-reduce.5.cloned.1.call-update
  16.8 42.1 %all-reduce.5.cloned.1.call-done = bf16[256,1,1152]{2,0,1:T(8,128)(2,1)} async-done(((bf16[256,1,1152]{2,0,1:T(8,128)(2,1)}), bf16[256,1,1152]{2,0,1:T(8,128)(2,1)}) %all-reduce.5.cloned.1.call-update) | async-done | bytes 589840 | tf_op jit(solution)/shard_map/psum | solution.py:82
  58.8 1.2 fusion.51
  60.1 0.5 broadcast.200
  60.6 1.0 reduce.23
  61.6 1.0 reshape.318
  62.6 3.8 %all-to-all-start = ((bf16[8,2,18432]{2,1,0:T(2,128)(2,1)}), bf16[8,2,18432]{2,1,0:T(2,128)(2,1)S(1)}, u32[]{:S(2)}, u32[]{:S(2)}) async-start(bf16[8,2,18432]{2,1,0:T(2,128)(2,1)} %reshape.318), calls=%async_computation | async-start | bytes 1179648 | tf_op jit(solution)/shard_map/all_to_all | solution.py:86
  66.4 0.2 all-reduce.7.cloned.1.call-start
  66.6 0.5 convolution_convert_fusion.6
  67.1 0.2 reshape.298
  67.3 9.5 %all-to-all-done = bf16[8,2,18432]{2,1,0:T(2,128)(2,1)S(1)} async-done(((bf16[8,2,18432]{2,1,0:T(2,128)(2,1)}), bf16[8,2,18432]{2,1,0:T(2,128)(2,1)S(1)}, u32[]{:S(2)}, u32[]{:S(2)}) %all-to-all-start) | async-done | bytes 589856 | tf_op jit(solution)/shard_map/all_to_all | solution.py:86
  76.8 0.6 reshape.319
  77.4 0.1 bitcast_convert_fusion.1
  77.5 0.7 bitcast_reduce_fusion
  78.2 0.7 multiply_reduce_fusion.1
  78.9 0.6 copy-done.26
  79.5 2.4 %fusion.28 = bf16[32,8,3,288]{3,1,2,0:T(8,128)(2,1)} fusion(bf16[2,1152,3,288]{1,3,2,0:T(8,128)(2,1)S(1)} %copy-done.26, f32[8,32,1,1152]{3,1,0,2:T(8,128)S(1)} %bitcast_convert_fusion.1, f32[1152]{0:T(1024)S(1)} %get-tuple-element.10, f32[1152]{0:T(1024)S(1)} %get-tuple-element.22, f32[32,8]{1,0:T(8,128)S(1)} %add_rsqrt_fusion, ...), kind=kOutput, calls=%fused_computation.38 | convolution fusion | flops 511303680 | bytes 3661824 | tf_op jit(solution)/shard_map/abd,dce->abce/dot_general | solution.py:26
  82.0 2.2 reshape.296
  84.1 1.0 fusion.132
  85.1 0.3 fusion.112
  85.4 2.3 fusion.134
  87.7 1.5 fusion.62
  89.2 1.9 fusion.60
  91.1 2.4 %fusion.61 = bf16[32,8,4,72]{3,1,2,0:T(8,128)(2,1)} fusion(f32[32,4,8,8]{2,3,1,0:T(8,128)S(1)} %fusion.112, bf16[32,8,1,4,72]{4,3,1,2,0:T(4,128)(2,1)S(1)} %copy-done.10, f32[32,4,8,8]{2,3,1,0:T(8,128)} %get-tuple-element.20, f32[32,4,8]{2,1,0:T(4,128)S(1)} %get-tuple-element.19), kind=kOutput, calls=%fused_computation.82 | convolution fusion | flops 1311751 | bytes 364544 | tf_op jit(solution)/shard_map/phfg,pfhd->pghd/dot_general | solution.py:62
  93.5 0.1 copy.77
  93.6 0.2 stack.26
  93.8 1.1 copy.75
  94.8 0.2 stack.25
  95.0 0.1 copy.74
  95.1 0.2 stack.24
  95.3 3.3 %fusion.4 = bf16[32,8,1152]{2,1,0:T(8,128)(2,1)} fusion(bf16[2,1152,3,288]{1,3,2,0:T(8,128)(2,1)} %param.9, bf16[32,8,1,288]{3,1,2,0:T(8,128)(2,1)S(1)} %bitcast.221, bf16[32,8,1,288]{3,1,2,0:T(8,128)(2,1)S(1)} %bitcast.222, bf16[32,8,1,288]{3,1,2,0:T(8,128)(2,1)S(1)} %bitcast.223), kind=kOutput, calls=%fused_computation.6 | convolution fusion | flops 510345216 | bytes 3022848 | tf_op jit(solution)/shard_map/abce,dce->abd/dot_general | solution.py:112
  98.6 37.1 %all-reduce.7.cloned.1.call-done = bf16[32,8,1152]{2,1,0:T(8,128)(2,1)} async-done(((bf16[32,8,1152]{2,1,0:T(8,128)(2,1)}), bf16[32,8,1152]{2,1,0:T(8,128)(2,1)}) %all-reduce.7.cloned.1.call-update) | async-done | bytes 589840 | tf_op jit(solution)/shard_map/psum | solution.py:82
  135.7 2.1 fusion.58
  137.9 0.9 fusion.50
  138.8 0.9 copy.81
  139.7 4.2 %all-to-all-start.1 = ((bf16[32,8,1152]{2,0,1:T(8,128)(2,1)}), bf16[32,8,1152]{2,0,1:T(8,128)(2,1)}, u32[]{:S(2)}, u32[]{:S(2)}) async-start(bf16[32,8,1152]{2,0,1:T(8,128)(2,1)} %copy.81), calls=%async_computation.1 | async-start | bytes 1179648 | tf_op jit(solution)/shard_map/all_to_all | solution.py:90
  143.9 0.3 all-reduce.9.cloned.1.call-start
  144.2 2.5 %fusion.59 = bf16[32,8,4,72]{3,1,2,0:T(8,128)(2,1)} fusion(bf16[32,8,1,4,72]{4,3,1,2,0:T(4,128)(2,1)S(1)} %get-tuple-element.16, f32[32,4,8]{2,1,0:T(4,128)S(1)} %get-tuple-element.19, bf16[32,8,1,4,72]{4,3,1,2,0:T(4,128)(2,1)} %get-tuple-element.15, bf16[32,8,1,4,72]{4,3,1,2,0:T(4,128)(2,1)} %copy-done.8), kind=kOutput, calls=%fused_computation.80 | convolution fusion | flops 2466823 | bytes 593920 | tf_op jit(solution)/shard_map/phfg,pghd->pfhd/dot_general | solution.py:37
  146.6 1.1 copy.71
  147.7 0.2 reshape.297
  147.9 1.3 convolution_convert_fusion
  149.2 5.2 %all-to-all-done.1 = bf16[32,8,1152]{2,0,1:T(8,128)(2,1)} async-done(((bf16[32,8,1152]{2,0,1:T(8,128)(2,1)}), bf16[32,8,1152]{2,0,1:T(8,128)(2,1)}, u32[]{:S(2)}, u32[]{:S(2)}) %all-to-all-start.1) | async-done | bytes 589856 | tf_op jit(solution)/shard_map/all_to_all | solution.py:90
  154.3 1.3 bitcast_convert_fusion
  155.6 0.2 copy-done.3
  155.8 0.4 convolution_convert_fusion.11
  156.2 0.4 copy-done.16
  156.7 1.4 convolution_convert_fusion.7
  158.1 1.4 fusion.117
  159.5 3.3 %convolution_convert_fusion.9 = bf16[4,72,256]{2,1,0:T(8,128)(2,1)} fusion(f32[4,256,256]{1,2,0:T(8,128)} %fusion.117, bf16[256,1,3,4,72]{0,4,3,2,1:T(8,128)(2,1)S(1)} %bitcast.229, f32[4,256,256]{1,2,0:T(8,128)} %get-tuple-element.18, f32[4,256]{1,0:T(4,128)S(1)} %copy-done.29), kind=kOutput, calls=%fused_computation.86 | convolution fusion | flops 39658752 | bytes 4497408 | tf_op jit(solution)/shard_map/fhpq,qfhd->pfhd/dot_general | solution.py:59
  162.8 3.3 %convolution_convert_fusion.8 = bf16[4,72,256]{2,1,0:T(8,128)(2,1)} fusion(f32[4,256,256]{1,2,0:T(8,128)} %fusion.117, bf16[256,1,3,4,72]{0,4,3,2,1:T(8,128)(2,1)S(1)} %bitcast.230, f32[4,256,256]{1,2,0:T(8,128)} %get-tuple-element.18, f32[4,256]{1,0:T(4,128)S(1)} %copy-done.29), kind=kOutput, calls=%fused_computation.85 | convolution fusion | flops 39658752 | bytes 4497408 | tf_op jit(solution)/shard_map/fhpq,pfhd->qfhd/dot_general | solution.py:62
  166.1 3.4 %fusion.7 = bf16[256,1,1152]{2,0,1:T(8,128)(2,1)} fusion(bf16[2,1152,3,288]{1,3,2,0:T(8,128)(2,1)} %param.9, bf16[256,1,1,288]{0,3,2,1:T(8,128)(2,1)S(1)} %bitcast.231, bf16[256,1,1,288]{0,3,2,1:T(8,128)(2,1)} %bitcast.233, bf16[256,1,1,288]{0,3,2,1:T(8,128)(2,1)} %bitcast.232), kind=kOutput, calls=%fused_computation.11 | convolution fusion | flops 510345216 | bytes 3022848 | tf_op jit(solution)/shard_map/abce,dce->abd/dot_general | solution.py:120
  169.5 54.3 %all-reduce.9.cloned.1.call-done = (bf16[32,8,1152]{2,1,0:T(8,128)(2,1)}, bf16[256,1,1152]{2,0,1:T(8,128)(2,1)}) async-done(((bf16[32,8,1152]{2,1,0:T(8,128)(2,1)}, bf16[256,1,1152]{2,0,1:T(8,128)(2,1)}), (bf16[32,8,1152]{2,1,0:T(8,128)(2,1)}, bf16[256,1,1152]{2,0,1:T(8,128)(2,1)})) %all-reduce.9.cloned.1.call-update) | async-done | bytes 1179664 | tf_op jit(solution)/shard_map/psum | solution.py:82
  223.8 2.6 %fusion.52 = bf16[32,8,1152]{2,1,0:T(8,128)(2,1)} fusion(bf16[32,8,1152]{2,1,0:T(8,128)(2,1)} %get-tuple-element.12, f32[8,32,1,1152]{3,1,0,2:T(8,128)S(1)} %bitcast_convert_fusion.1, f32[1152]{0:T(1024)S(1)} %copy-done.18), kind=kLoop, calls=%fused_computation.65 | loop fusion | flops 1179648 | bytes 2363904 | tf_op jit(solution)/shard_map/convert_element_type | solution.py:106
  226.5 0.4 fusion.57
  226.9 1.3 fusion.47
  (67 shorter events, 0.2 us)
Async XLA Ops:
  7.2 2.8 %copy-start = (bf16[256,1,1152]{2,0,1:T(8,128)(2,1)S(1)}, bf16[256,1,1152]{2,0,1:T(8,128)(2,1)}, u32[]{:S(2)}) copy-start(bf16[256,1,1152]{2,0,1:T(8,128)(2,1)} %param.7) | copy-start | bytes 1769476
  7.2 2.7 %copy-start.24 = (f32[2,1152]{1,0:T(2,128)S(1)}, f32[2,1152]{1,0:T(2,128)}, u32[]{:S(2)}) copy-start(f32[2,1152]{1,0:T(2,128)} %param.12) | copy-start | bytes 27652
  7.2 2.7 %copy-start.23 = (f32[2,1152]{1,0:T(2,128)S(1)}, f32[2,1152]{1,0:T(2,128)}, u32[]{:S(2)}) copy-start(f32[2,1152]{1,0:T(2,128)} %param.11) | copy-start | bytes 27652
  7.2 51.6 %all-reduce.5.cloned.1.call-start = ((), (), s32[]{:S(2)}) async-start(), calls=%async_computation.2 | async-start | bytes 1179648 | tf_op jit(solution)/shard_map/psum | solution.py:82
  8.5 3.9 %copy-start.19 = (f32[256]{0:T(256)}, f32[256]{0:T(256)S(1)}, u32[]{:S(2)}) copy-start(f32[256]{0:T(256)S(1)} %broadcast_multiply_fusion.5) | copy-start | bytes 3076
  9.9 2.6 %copy-start.21 = (f32[256]{0:T(256)}, f32[256]{0:T(256)S(1)}, u32[]{:S(2)}) copy-start(f32[256]{0:T(256)S(1)} %add_rsqrt_fusion.1) | copy-start | bytes 3076
  10.0 2.5 %copy-start.11 = (f32[1152]{0:T(1024)}, f32[1152]{0:T(1024)S(1)}, u32[]{:S(2)}) copy-start(f32[1152]{0:T(1024)S(1)} %get-tuple-element.21) | copy-start | bytes 13828
  12.5 2.2 copy-start.15
  14.0 0.7 copy-start.28
  14.0 1.3 copy-start.1
  14.7 1.9 copy-start.25
  16.7 43.3 %copy-start.13 = (f32[1152]{0:T(1024)}, f32[1152]{0:T(1024)S(1)}, u32[]{:S(2)}) copy-start(f32[1152]{0:T(1024)S(1)} %get-tuple-element.7) | copy-start | bytes 13828
  16.7 49.9 %copy-start.17 = (f32[1152]{0:T(1024)}, f32[1152]{0:T(1024)S(1)}, u32[]{:S(2)}) copy-start(f32[1152]{0:T(1024)S(1)} %get-tuple-element.6) | copy-start | bytes 13828
  62.6 4.0 %copy-start.6 = (bf16[32,8,1152]{2,1,0:T(8,128)(2,1)S(1)}, bf16[32,8,1152]{2,1,0:T(8,128)(2,1)}, u32[]{:S(2)}) copy-start(bf16[32,8,1152]{2,1,0:T(8,128)(2,1)} %param.8) | copy-start | bytes 1769476
  62.6 14.2 %all-to-all-start = ((bf16[8,2,18432]{2,1,0:T(2,128)(2,1)}), bf16[8,2,18432]{2,1,0:T(2,128)(2,1)S(1)}, u32[]{:S(2)}, u32[]{:S(2)}) async-start(bf16[8,2,18432]{2,1,0:T(2,128)(2,1)} %reshape.318), calls=%async_computation | async-start | bytes 1179648 | tf_op jit(solution)/shard_map/all_to_all | solution.py:86
  66.4 69.3 %all-reduce.7.cloned.1.call-start = ((), (), s32[]{:S(2)}) async-start(), calls=%async_computation.3 | async-start | bytes 1179648 | tf_op jit(solution)/shard_map/psum | solution.py:82
  77.4 2.1 copy-start.26
  85.1 2.5 %copy-start.8 = (bf16[32,8,1,4,72]{4,3,1,2,0:T(4,128)(2,1)}, bf16[32,8,1,4,72]{4,3,1,2,0:T(4,128)(2,1)S(1)}, u32[]{:S(2)}) copy-start(bf16[32,8,1,4,72]{4,3,1,2,0:T(4,128)(2,1)S(1)} %get-tuple-element.14) | copy-start | bytes 442372
  85.1 2.6 %copy-start.9 = (bf16[32,8,1,4,72]{4,3,1,2,0:T(4,128)(2,1)S(1)}, bf16[32,8,1,4,72]{4,3,1,2,0:T(4,128)(2,1)}, u32[]{:S(2)}) copy-start(bf16[32,8,1,4,72]{4,3,1,2,0:T(4,128)(2,1)} %get-tuple-element.15) | copy-start | bytes 442372
  89.2 1.9 copy-start.10
  98.6 39.3 %copy-start.7 = (bf16[32,8,1152]{2,1,0:T(8,128)(2,1)S(1)}, bf16[32,8,1152]{2,1,0:T(8,128)(2,1)}, u32[]{:S(2)}) copy-start(bf16[32,8,1152]{2,1,0:T(8,128)(2,1)} %param.8) | copy-start | bytes 1769476
  135.7 2.1 copy-start.4
  139.7 14.7 %all-to-all-start.1 = ((bf16[32,8,1152]{2,0,1:T(8,128)(2,1)}), bf16[32,8,1152]{2,0,1:T(8,128)(2,1)}, u32[]{:S(2)}, u32[]{:S(2)}) async-start(bf16[32,8,1152]{2,0,1:T(8,128)(2,1)} %copy.81), calls=%async_computation.1 | async-start | bytes 1179648 | tf_op jit(solution)/shard_map/all_to_all | solution.py:90
  143.9 4.0 %copy-start.2 = (bf16[2,288,1152]{2,1,0:T(8,128)(2,1)S(1)}, bf16[2,288,1152]{2,1,0:T(8,128)(2,1)}, u32[]{:S(2)}) copy-start(bf16[2,288,1152]{2,1,0:T(8,128)(2,1)} %param.10) | copy-start | bytes 3981316
  143.9 79.9 %all-reduce.9.cloned.1.call-start = ((), (), s32[]{:S(2)}) async-start(), calls=%async_computation.4 | async-start | bytes 2359296 | tf_op jit(solution)/shard_map/psum | solution.py:82
  149.2 6.5 %copy-start.14 = (f32[1152]{0:T(1024)S(1)}, f32[1152]{0:T(1024)}, u32[]{:S(2)}) copy-start(f32[1152]{0:T(1024)} %copy-done.13) | copy-start | bytes 13828
  154.3 1.5 copy-start.3
  155.6 1.1 copy-start.16
  155.6 1.1 copy-start.29
  162.8 3.3 %copy-start.27 = (bf16[4,72,256]{2,1,0:T(8,128)(2,1)S(1)}, bf16[4,72,256]{2,1,0:T(8,128)(2,1)}, u32[]{:S(2)}) copy-start(bf16[4,72,256]{2,1,0:T(8,128)(2,1)} %convolution_convert_fusion.7) | copy-start | bytes 442372
  169.5 54.3 %copy-start.18 = (f32[1152]{0:T(1024)S(1)}, f32[1152]{0:T(1024)}, u32[]{:S(2)}) copy-start(f32[1152]{0:T(1024)} %copy-done.17) | copy-start | bytes 13828
  223.8 2.6 %copy-start.5 = (bf16[256,1,1152]{2,0,1:T(8,128)(2,1)S(1)}, bf16[256,1,1152]{2,0,1:T(8,128)(2,1)}, u32[]{:S(2)}) copy-start(bf16[256,1,1152]{2,0,1:T(8,128)(2,1)} %get-tuple-element.13) | copy-start | bytes 1769476
  223.8 2.6 %copy-start.12 = (f32[1152]{0:T(1024)S(1)}, f32[1152]{0:T(1024)}, u32[]{:S(2)}) copy-start(f32[1152]{0:T(1024)} %copy-done.11) | copy-start | bytes 13828
  223.8 2.6 %copy-start.20 = (f32[256]{0:T(256)S(1)}, f32[256]{0:T(256)}, u32[]{:S(2)}) copy-start(f32[256]{0:T(256)} %copy-done.19) | copy-start | bytes 3076
  223.8 2.6 %copy-start.22 = (f32[256]{0:T(256)S(1)}, f32[256]{0:T(256)}, u32[]{:S(2)}) copy-start(f32[256]{0:T(256)} %copy-done.21) | copy-start | bytes 3076
Sparse Core Ops, SparseCore 0:
  16.8 41.9 all-reduce.4
  98.7 36.9 all-reduce.6
  169.6 54.1 all-reduce.8
where the time goes:
time: 236 us; the launch traced here: 235 us
  waiting for transfers between devices  148 us (63%)
  matrix products  37.4 us (16%)
  other arithmetic  15.1 us (6%)
  between operations  14.3 us (6%)
  local copies, waits for them, and re-layouts  11.3 us (5%)
  starting transfers between devices  8.52 us (4%)
    psum x3, waiting for transfers between devices, head_total(): lax.psum(partial_value.astype(jnp.bfloat16), 'tp').astype(jnp.float32)  133 us
    all_to_all x1, waiting for transfers between devices, to_patches(): lax.all_to_all(frame_rows, 'seq', split_axis=0, concat_axis=1, tiled=True)  9.52 us
    dot_general x2, matrix products, attend_back(): jnp.einsum(layout_forms[2], grad_scores, queries, preferred_element_type=...  5.7 us
    dot_general x2, matrix products, attend_back(): jnp.einsum(layout_forms[1], grad_scores, key_heads, preferred_element_typ...  5.19 us
    all_to_all x1, waiting for transfers between devices, to_frames(): lax.all_to_all(patch_rows, 'seq', split_axis=1, concat_axis=0, tiled=True)  5.18 us
    dot_general x2, matrix products, attend(): jnp.einsum('abd,dce->abce', modded, qkv_weights, preferred_element_type=j...  4.86 us
  transfers between devices with their start and end apart: 5, of which 5 were waited for; matrix products, arithmetic and copies ran while one was open for 2% of the time, Pallas kernels for 0%

commit v1 on v0

v1 whole, which is shorter than its diff:
```python
import functools
import math

import jax
import jax.numpy as jnp
from jax import lax
from jax.experimental import pallas as pl
from jax.experimental.pallas import tpu as pltpu
from jax.sharding import PartitionSpec as P

HEAD_DIM = 72
BF16 = jnp.bfloat16
F32 = jnp.float32
MESH = pl.DeviceIdType.MESH
VMEM = pl.BlockSpec(memory_space=pltpu.VMEM)
LIMIT = 48 * 1024 * 1024


def dot_nn(a, b):
    return lax.dot_general(a, b, (((1,), (0,)), ((), ())), preferred_element_type=F32)


def dot_nt(a, b):
    return lax.dot_general(a, b, (((1,), (1,)), ((), ())), preferred_element_type=F32)


def dot_tn(a, b):
    return lax.dot_general(a, b, (((0,), (0,)), ((), ())), preferred_element_type=F32)


def normalize(rows):
    widened = rows.astype(F32)
    center = widened - jnp.mean(widened, axis=-1, keepdims=True)
    inv_std = lax.rsqrt(jnp.mean(center * center, axis=-1, keepdims=True) + 1e-06)
    return center * inv_std, inv_std


def project(rows, shift_ref, scale_ref, weight_ref):
    normed, _ = normalize(rows)
    modded = (normed * (1.0 + scale_ref[...]) + shift_ref[...]).astype(BF16)
    return tuple(dot_nn(modded, weight_ref[c]).astype(BF16) for c in range(3))


def head_masks(width):
    lane = lax.broadcasted_iota(jnp.int32, (1, width), 1)
    return [
        (lane >= h * HEAD_DIM) & (lane < (h + 1) * HEAD_DIM) for h in range(width // HEAD_DIM)
    ]


def pick(mask, value):
    return jnp.where(mask, value, jnp.zeros_like(value))


def head_probs(queries, keys, mask, same):
    scores = dot_nt(pick(mask, queries), keys) * (1.0 / math.sqrt(HEAD_DIM))
    if same is not None:
        scores = jnp.where(same, scores, -jnp.inf)
    shifted = jnp.exp(scores - jnp.max(scores, axis=-1, keepdims=True))
    return shifted / jnp.sum(shifted, axis=-1, keepdims=True)


def same_patch(total, seqs, part):
    row = lax.broadcasted_iota(jnp.int32, (total, total), 0)
    col = lax.broadcasted_iota(jnp.int32, (total, total), 1)
    block = seqs * part
    return (row // block == col // block) & (row % part == col % part)


def backward_heads(queries, keys, values, grad_attn, probs_of):
    masks = head_masks(queries.shape[1])
    grads = [jnp.zeros(queries.shape, F32) for _ in range(3)]
    for h, mask in enumerate(masks):
        probs = probs_of(h, mask)
        grad_probs = dot_nt(pick(mask, grad_attn), values)
        mean = jnp.sum(probs * grad_probs, axis=-1, keepdims=True)
        grad_scores = (probs * (grad_probs - mean) * (1.0 / math.sqrt(HEAD_DIM))).astype(BF16)
        grads[0] = jnp.where(mask, dot_nn(grad_scores, keys), grads[0])
        grads[1] = jnp.where(mask, dot_tn(grad_scores, queries), grads[1])
        grads[2] = jnp.where(mask, dot_tn(probs.astype(BF16), grad_attn), grads[2])
    return [grad.astype(BF16) for grad in grads]


def back_project(grads, weight_ref):
    total = dot_nt(grads[0], weight_ref[0])
    total += dot_nt(grads[1], weight_ref[1])
    return total + dot_nt(grads[2], weight_ref[2])


def as_rows(ref):
    return ref[...].astype(F32).reshape(-1, ref.shape[-1])


def put(ref, value):
    ref[...] = value.reshape(ref.shape).astype(BF16)


def spatial_forward(x_ref, shift_ref, scale_ref, weight_ref, out_ref, part_ref, qkv_ref):
    queries, keys, values = project(as_rows(x_ref), shift_ref, scale_ref, weight_ref)
    attended = jnp.zeros(queries.shape, F32)
    for mask in head_masks(queries.shape[1]):
        probs = head_probs(queries, keys, mask, None).astype(BF16)
        attended = jnp.where(mask, dot_nn(probs, values), attended)
    put(part_ref, dot_nn(attended.astype(BF16), out_ref[...]))
    for c, item in enumerate((queries, keys, values)):
        qkv_ref[c] = item


def grad_of_attended(g_ref, gate_ref, out_ref):
    grad_proj = (gate_ref[...] * as_rows(g_ref)).astype(BF16)
    return dot_nt(grad_proj, out_ref[...]).astype(BF16)


def spatial_backward(g_ref, gate_ref, weight_ref, out_ref, qkv_ref, part_ref):
    queries, keys, values = (qkv_ref[c] for c in range(3))
    grad_attn = grad_of_attended(g_ref, gate_ref, out_ref)
    grads = backward_heads(
        queries, keys, values, grad_attn, lambda h, mask: head_probs(queries, keys, mask, None)
    )
    put(part_ref, back_project(grads, weight_ref))


def temporal(
    x_ref, g_ref, shift_ref, scale_ref, gate_ref, weight_ref, out_ref, part_ref, gpart_ref
):
    _, seqs, part, _ = x_ref.shape
    queries, keys, values = project(as_rows(x_ref), shift_ref, scale_ref, weight_ref)
    same = same_patch(queries.shape[0], seqs, part)
    grad_attn = grad_of_attended(g_ref, gate_ref, out_ref)
    probs = []
    attended = jnp.zeros(queries.shape, F32)
    for mask in head_masks(queries.shape[1]):
        probs.append(head_probs(queries, keys, mask, same))
        attended = jnp.where(mask, dot_nn(probs[-1].astype(BF16), values), attended)
    put(part_ref, dot_nn(attended.astype(BF16), out_ref[...]))
    grads = backward_heads(queries, keys, values, grad_attn, lambda h, mask: probs[h])
    put(gpart_ref, back_project(grads, weight_ref))


def forward_end(total, x_ref, c, gate_ref):
    return (x_ref[c].astype(F32) + gate_ref[...] * total).astype(BF16)


def backward_end(total, x_ref, c, g_ref, scale_ref):
    normed, inv_std = normalize(x_ref[c])
    grad_norm = total * (1.0 + scale_ref[...])
    back = inv_std * (
        grad_norm
        - jnp.mean(grad_norm, axis=-1, keepdims=True)
        - normed * jnp.mean(grad_norm * normed, axis=-1, keepdims=True)
    )
    return (g_ref[c].astype(F32) + back).astype(BF16)


def head_sums(parts, totals, ends, moved, scratch, seqs, tps):
    inbox, halves, others, sems, seq_sems, own_sem = scratch
    s, z = lax.axis_index("seq"), lax.axis_index("tp")
    chunks = parts[0].shape[0]
    inner = (z > 0) & (z < tps - 1)
    outer = jnp.logical_not(inner)
    near = jnp.where(z < tps // 2, z + 1, z - 1)
    far = jnp.where(z < tps // 2, z - 1, z + 1)
    across = near
    barrier = pltpu.get_barrier_semaphore()

    def greet(tp):
        pl.semaphore_signal(barrier, inc=1, device_id=(s, tp), device_id_type=MESH)

    greet(near)

    @pl.when(inner)
    def _():
        greet(far)

    any_moved = any(item is not None for item in moved)
    if any_moved:

        @pl.loop(1, seqs)
        def _(k):
            pl.semaphore_signal(
                barrier, inc=1, device_id=(lax.rem(s + k, seqs), z), device_id_type=MESH
            )

    peers = seqs - 1 if any_moved else 0

    @pl.when(inner)
    def _():
        pl.semaphore_wait(barrier, 2 + peers)

    @pl.when(outer)
    def _():
        pl.semaphore_wait(barrier, 1 + peers)

    items = [(i, c) for c in range(chunks) for i in range(len(parts))]

    def remote(src, dst, kind, i, c, tp):
        return pltpu.make_async_remote_copy(
            src_ref=src.at[c],
            dst_ref=dst.at[c],
            send_sem=sems.at[kind, 0, i, c],
            recv_sem=sems.at[kind, 1, i, c],
            device_id=(s, tp),
            device_id_type=MESH,
        )

    def inward(i, c):
        return remote(parts[i], inbox.at[i], 0, i, c, near)

    def cross(i, c):
        return remote(halves.at[i], others.at[i], 1, i, c, across)

    def outward(i, c):
        return remote(totals[i], totals[i], 2, i, c, far)

    def spread(i, c):
        @pl.loop(1, seqs)
        def _(k):
            to = lax.rem(s + k, seqs)
            pltpu.make_async_remote_copy(
                src_ref=totals[i].at[c, to],
                dst_ref=moved[i].at[c, s],
                send_sem=seq_sems.at[0, c],
                recv_sem=seq_sems.at[1, c],
                device_id=(to, z),
                device_id_type=MESH,
            ).start()

        pltpu.make_async_copy(totals[i].at[c, s], moved[i].at[c, s], own_sem.at[c]).start()

    @pl.when(outer)
    def _():
        for i, c in items:
            inward(i, c).start()
        for i, c in items:
            outward(i, c).wait_recv()
            if moved[i] is not None:
                spread(i, c)
        for i, c in items:
            inward(i, c).wait_send()

    @pl.when(inner)
    def _():
        def fold(i, c):
            inward(i, c).wait_recv()
            halves[i, c] = (parts[i][c].astype(F32) + inbox[i, c].astype(F32)).astype(BF16)
            cross(i, c).start()

        def finish(i, c):
            cross(i, c).wait_recv()
            total = halves[i, c].astype(F32) + others[i, c].astype(F32)
            totals[i][c] = ends[i](total, c)
            outward(i, c).start()
            if moved[i] is not None:
                spread(i, c)

        lead = 2
        for at in range(len(items) + lead):
            if at < len(items):
                fold(*items[at])
            if at >= lead:
                finish(*items[at - lead])
        for i, c in items:
            cross(i, c).wait_send()
            outward(i, c).wait_send()

    for i, c in items:
        if moved[i] is not None:
            pltpu.make_async_copy(totals[i].at[c, s], moved[i].at[c, s], own_sem.at[c]).wait()
            rest = pl.ds(0, seqs - 1)
            both = pltpu.make_async_remote_copy(
                src_ref=totals[i].at[c, rest],
                dst_ref=moved[i].at[c, rest],
                send_sem=seq_sems.at[0, c],
                recv_sem=seq_sems.at[1, c],
                device_id=(lax.rem(s + 1, seqs), z),
                device_id_type=MESH,
            )
            both.wait_send()
            both.wait_recv()


def middle_kernel(seqs, tps, part_ref, x_ref, gate_ref, mid_ref, total, *scratch):
    ends = [lambda value, c: forward_end(value, x_ref, c, gate_ref)]
    head_sums([part_ref], [total], ends, [mid_ref], scratch, seqs, tps)


def temporal_sums(
    seqs, tps, gpart_ref, part_ref, x_ref, g_ref, gate_ref, scale_ref, result_ref, back_ref,
    total, *scratch
):
    ends = [
        lambda value, c: backward_end(value, x_ref, c, g_ref, scale_ref),
        lambda value, c: forward_end(value, x_ref, c, gate_ref),
    ]
    head_sums(
        [gpart_ref, part_ref], [total, result_ref], ends, [back_ref, None], scratch, seqs, tps
    )


def spatial_sums(seqs, tps, gpart_ref, x_ref, g_ref, scale_ref, grad_ref, *scratch):
    ends = [lambda value, c: backward_end(value, x_ref, c, g_ref, scale_ref)]
    head_sums([gpart_ref], [grad_ref], ends, [None], scratch, seqs, tps)


def compute(body, outs, *operands):
    return pl.pallas_call(
        body,
        out_shape=outs,
        in_specs=[VMEM] * len(operands),
        out_specs=jax.tree.map(lambda _: VMEM, outs),
        compiler_params=pltpu.CompilerParams(vmem_limit_bytes=LIMIT),
    )(*operands)


def exchange(body, ident, outs, streams, own_total, seqs, tps, *operands):
    shape = operands[0].shape
    chunks = shape[0]
    scratch = [pltpu.VMEM(shape, BF16)] if own_total else []
    scratch += [pltpu.VMEM((streams, *shape), BF16)] * 3
    scratch += [
        pltpu.SemaphoreType.DMA((3, 2, streams, chunks)),
        pltpu.SemaphoreType.DMA((2, chunks)),
        pltpu.SemaphoreType.DMA((chunks,)),
    ]
    return pl.pallas_call(
        functools.partial(body, seqs, tps),
        out_shape=outs,
        in_specs=[VMEM] * len(operands),
        out_specs=jax.tree.map(lambda _: VMEM, outs),
        scratch_shapes=scratch,
        compiler_params=pltpu.CompilerParams(
            collective_id=ident, has_side_effects=True, vmem_limit_bytes=LIMIT
        ),
    )(*operands)


def per_device(
    seqs, tps, tokens, grad_out, qkv_weight, out_weight, mod_shift, mod_scale, mod_gate
):
    width = tokens.shape[-1]
    patches = tokens.shape[0] // seqs
    chunks = max(1, patches // 8)
    part = patches // chunks
    dims = (chunks, seqs, part, width)
    array = jax.ShapeDtypeStruct(dims, BF16)
    weights = jnp.transpose(qkv_weight, (0, 2, 1, 3))
    rows = [[item[b : b + 1] for b in range(2)] for item in (mod_shift, mod_scale, mod_gate)]
    shift, scale, gate = rows
    x = tokens.reshape(seqs, chunks, part, width).transpose(1, 0, 2, 3)
    g = grad_out.reshape(chunks, part, seqs, width).transpose(0, 2, 1, 3)

    cached = jax.ShapeDtypeStruct((3, tokens.shape[0], out_weight.shape[1]), BF16)
    part_s, qkv_s = compute(
        spatial_forward, (array, cached), x, shift[0], scale[0], weights[0], out_weight[0]
    )
    mid = exchange(middle_kernel, 0, array, 1, True, seqs, tps, part_s, x, gate[0])
    part_t, gpart_t = compute(
        temporal, (array, array), mid, g, shift[1], scale[1], gate[1], weights[1], out_weight[1]
    )
    result, grad_mid = exchange(
        temporal_sums, 1, (array, array), 2, True, seqs, tps,
        gpart_t, part_t, mid, g, gate[1], scale[1],
    )
    gpart_s = compute(
        spatial_backward, array, grad_mid, gate[0], weights[0], out_weight[0], qkv_s
    )
    grad_in = exchange(spatial_sums, 2, array, 1, False, seqs, tps, gpart_s, x, grad_mid, scale[0])
    result = result.transpose(0, 2, 1, 3).reshape(grad_out.shape)
    return (result, grad_in.transpose(1, 0, 2, 3).reshape(tokens.shape))


def solution(mesh):
    in_specs = (
        P(None, "seq", None),
        P("seq", None, None),
        P(None, None, None, "tp"),
        P(None, "tp", None),
        P(),
        P(),
        P(),
    )
    out_specs = (P("seq", None, None), P(None, "seq", None))
    return jax.shard_map(
        functools.partial(per_device, mesh.shape["seq"], mesh.shape["tp"]),
        mesh=mesh,
        in_specs=in_specs,
        out_specs=out_specs,
        check_vma=False,
    )
```

time: 236 us -> 130 us (0.55)
  waiting for transfers between devices: 148 us -> 0 us
  Pallas kernels: 0 us -> 115 us
  matrix products: 37.4 us -> 0 us
  other arithmetic: 15.1 us -> 0 us
  between operations: 14.3 us -> 0.76 us
  starting transfers between devices: 8.52 us -> 0 us
    psum x3 -> x0, waiting for transfers between devices: 133 us -> none  [head_total(): lax.psum(partial_value.astype(jnp.bfloat16), 'tp').astype(jnp.float32)]
    pallas_call x0 -> x6, Pallas kernels: none -> 115 us  [the longest x3 101 us: exchange(): pl.pallas_call(functools.partial(body, seqs, tps), out_shape=outs, in_spe...]
    dot_general x18 -> x0, matrix products: 33.6 us -> none  [the longest x2 5.7 us: attend_back(): jnp.einsum(layout_forms[2], grad_scores, queries, preferred_element_type=...]
    all_to_all x2 -> x0, waiting for transfers between devices: 14.7 us -> none  [the longest x1 9.52 us: to_patches(): lax.all_to_all(frame_rows, 'seq', split_axis=0, concat_axis=1, tiled=True)]
    convert_element_type x7 -> x0, other arithmetic: 8.44 us -> none  [the longest x1 2.61 us: per_device(): (mid_patch.astype(jnp.float32) + mod_gate[1] * head_total(partial_t)).ast...]
    all_to_all x2 -> x0, starting transfers between devices: 8 us -> none  [the longest x1 4.21 us: to_frames(): lax.all_to_all(patch_rows, 'seq', split_axis=1, concat_axis=0, tiled=True)]
    reduce_sum x6 -> x0, other arithmetic: 6.52 us -> none  [the longest x2 2.49 us: norm_back(): jnp.mean(grad_norm, axis=-1, keepdims=True)]
    unnamed x62 -> x9, local copies, waits for them, and re-layouts: 3.49 us -> 7.53 us
  transfers between devices with their start and end apart: 5 -> 0, of which waited for: 5 -> 0; matrix products, arithmetic and copies ran while one was open for 2% -> 0% of each run, Pallas kernels for 0% -> 0%
where the time goes in v1:
time: 130 us
  Pallas kernels  115 us (88%)
  local copies, waits for them, and re-layouts  13.5 us (10%)
    pallas_call x3, Pallas kernels, exchange(): pl.pallas_call(functools.partial(body, seqs, tps), out_shape=outs, in_spe...  101 us
    pallas_call x3, Pallas kernels, compute(): pl.pallas_call(body, out_shape=outs, in_specs=[VMEM] * len(operands), out...  14.1 us
    unnamed x9, local copies, waits for them, and re-layouts  7.53 us
    squeeze x1, local copies, waits for them, and re-layouts, per_device(): weights[1]  3.18 us

profile of v1, /device:TPU:0, one launch (start us, length us, event | category | flops | bytes accessed | tf_op | source)
XLA Modules:
  0.0 129.6 jit_solution(2531885636183591145)
XLA Ops:
  0.6 0.8 fusion.1
  1.4 6.6 %copy.11 = bf16[2,1152,3,288]{3,1,2,0:T(8,128)(2,1)} copy(bf16[2,1152,3,288]{1,3,2,0:T(8,128)(2,1)} %param.9) | data formatting | bytes 7962624 | tf_op args[2]
  8.0 0.0 copy-start
  8.0 3.2 %slice_bitcast_fusion = (bf16[3,1152,288]{2,1,0:T(8,128)(2,1)S(1)}, bf16[3,1152,288]{2,1,0:T(8,128)(2,1)S(1)}) fusion(bf16[2,3,1152,288]{3,2,1,0:T(8,128)(2,1)} %bitcast.28), kind=kLoop, calls=%fused_computation | loop fusion | bytes 7962624 | tf_op jit(solution)/shard_map/squeeze | solution.py:358
  11.2 0.0 copy-start.1
  11.2 0.0 copy-done
  11.2 0.1 slice_bitcast_fusion.2
  11.3 0.0 copy-start.3
  11.4 0.9 copy-done.1
  12.3 0.0 copy-start.2
  12.3 3.2 %shard_map.86 = (bf16[4,8,8,1152]{3,2,1,0:T(8,128)(2,1)S(1)}, bf16[3,256,288]{2,1,0:T(8,128)(2,1)S(1)}) custom-call(bf16[4,8,8,1152]{3,2,1,0:T(8,128)(2,1)S(1)} %bitcast.21, f32[1,1152]{1,0:T(1,128)S(1)} %get-tuple-element.24.shift_ref, f32[1,1152]{1,0:T(1,128)S(1)} %get-tuple-element.21.scale_ref, bf16[3,1152,288]{2,1,0:T(8,128)(2,1)S(1)} %get-tuple-element.15.weight_ref, ...), custom_call_target="tpu_custom_call" | custom-call | tf_op jit(solution)/shard_map/pallas_call | solution.py:306
  15.6 0.0 copy-done.3
  15.6 33.3 %shard_map.87.x_ref = bf16[4,8,8,1152]{3,2,1,0:T(8,128)(2,1)S(1)} custom-call(bf16[4,8,8,1152]{3,2,1,0:T(8,128)(2,1)S(1)} %get-tuple-element.8.part_ref, bf16[4,8,8,1152]{3,2,1,0:T(8,128)(2,1)S(1)} %bitcast.22, f32[1,1152]{1,0:T(1,128)S(1)} %get-tuple-element.19.gate_ref), custom_call_target="tpu_custom_call" | custom-call | tf_op jit(solution)/shard_map/pallas_call | solution.py:325
  48.9 0.0 copy-done.2
  48.9 0.1 copy.17
  49.0 6.3 %shard_map.88 = (bf16[4,8,8,1152]{3,2,1,0:T(8,128)(2,1)S(1)}, bf16[4,8,8,1152]{3,2,1,0:T(8,128)(2,1)S(1)}) custom-call(bf16[4,8,8,1152]{3,2,1,0:T(8,128)(2,1)S(1)} %shard_map.87.x_ref, bf16[4,8,8,1152]{3,2,1,0:T(8,128)(2,1)S(1)} %bitcast.24, f32[1,1152]{1,0:T(1,128)S(1)} %get-tuple-element.25.shift_ref, f32[1,1152]{1,0:T(1,128)S(1)} %get-tuple-element.20.scale_ref, ...), custom_call_target="tpu_custom_call" | custom-call | tf_op jit(solution)/shard_map/pallas_call | solution.py:306
  55.4 41.6 %shard_map.89 = (bf16[4,8,8,1152]{3,2,1,0:T(8,128)(2,1)S(1)}, bf16[4,8,8,1152]{3,2,1,0:T(8,128)(2,1)S(1)}) custom-call(bf16[4,8,8,1152]{3,2,1,0:T(8,128)(2,1)S(1)} %get-tuple-element.9.gpart_ref, bf16[4,8,8,1152]{3,2,1,0:T(8,128)(2,1)S(1)} %get-tuple-element.10.part_ref, bf16[4,8,8,1152]{3,2,1,0:T(8,128)(2,1)S(1)} %shard_map.87.x_ref, ...), custom_call_target="tpu_custom_call" | custom-call | tf_op jit(solution)/shard_map/pallas_call | solution.py:325
  97.0 4.5 %shard_map.90.gpart_ref = bf16[4,8,8,1152]{3,2,1,0:T(8,128)(2,1)S(1)} custom-call(bf16[4,8,8,1152]{3,2,1,0:T(8,128)(2,1)S(1)} %get-tuple-element.12.g_ref, f32[1,1152]{1,0:T(1,128)S(1)} %get-tuple-element.19.gate_ref, bf16[3,1152,288]{2,1,0:T(8,128)(2,1)S(1)} %get-tuple-element.15.weight_ref, bf16[288,1152]{1,0:T(8,128)(2,1)S(1)} %get-tuple-element.17.out_ref, ...), custom_call_target="tpu_custom_call" | custom-call | tf_op jit(solution)/shard_map/pallas_call | solution.py:306
  101.5 26.3 %shard_map.91 = bf16[4,8,8,1152]{3,2,1,0:T(8,128)(2,1)S(1)} custom-call(bf16[4,8,8,1152]{3,2,1,0:T(8,128)(2,1)S(1)} %shard_map.90.gpart_ref, bf16[4,8,8,1152]{3,2,1,0:T(8,128)(2,1)S(1)} %bitcast.23, bf16[4,8,8,1152]{3,2,1,0:T(8,128)(2,1)S(1)} %get-tuple-element.12.g_ref, f32[1,1152]{1,0:T(1,128)S(1)} %get-tuple-element.21.scale_ref), custom_call_target="tpu_custom_call" | custom-call | tf_op jit(solution)/shard_map/pallas_call | solution.py:325
  127.8 0.9 copy.14
  128.7 0.9 copy.13
  (2 shorter events, 0.1 us)
Async XLA Ops:
  8.0 3.2 %copy-start = (bf16[2,288,1152]{2,1,0:T(8,128)(2,1)S(1)}, bf16[2,288,1152]{2,1,0:T(8,128)(2,1)}, u32[]{:S(2)}) copy-start(bf16[2,288,1152]{2,1,0:T(8,128)(2,1)} %param.10) | copy-start | bytes 3981316
  11.2 1.1 copy-start.1
  11.3 4.2 %copy-start.3 = (f32[2,1152]{1,0:T(2,128)S(1)}, f32[2,1152]{1,0:T(2,128)}, u32[]{:S(2)}) copy-start(f32[2,1152]{1,0:T(2,128)} %param.13) | copy-start | bytes 27652
  12.3 36.6 %copy-start.2 = (bf16[32,8,1152]{2,1,0:T(8,128)(2,1)S(1)}, bf16[32,8,1152]{2,1,0:T(8,128)(2,1)}, u32[]{:S(2)}) copy-start(bf16[32,8,1152]{2,1,0:T(8,128)(2,1)} %param.8) | copy-start | bytes 1769476

commit v2 on v1

v2 whole, which is shorter than its diff:
```python
import functools
import math

import jax
import jax.numpy as jnp
from jax import lax
from jax.experimental import pallas as pl
from jax.experimental.pallas import tpu as pltpu
from jax.sharding import PartitionSpec as P

HEAD_DIM = 72
BF16 = jnp.bfloat16
F32 = jnp.float32
MESH = pl.DeviceIdType.MESH
VMEM = pl.BlockSpec(memory_space=pltpu.VMEM)
LIMIT = 48 * 1024 * 1024


def dot_nn(a, b):
    return lax.dot_general(a, b, (((1,), (0,)), ((), ())), preferred_element_type=F32)


def dot_nt(a, b):
    return lax.dot_general(a, b, (((1,), (1,)), ((), ())), preferred_element_type=F32)


def dot_tn(a, b):
    return lax.dot_general(a, b, (((0,), (0,)), ((), ())), preferred_element_type=F32)


def normalize(rows):
    widened = rows.astype(F32)
    center = widened - jnp.mean(widened, axis=-1, keepdims=True)
    inv_std = lax.rsqrt(jnp.mean(center * center, axis=-1, keepdims=True) + 1e-06)
    return center * inv_std, inv_std


def project(rows, shift_ref, scale_ref, weight_ref, b):
    normed, _ = normalize(rows)
    modded = (normed * (1.0 + scale_ref[b : b + 1]) + shift_ref[b : b + 1]).astype(BF16)
    return tuple(dot_nn(modded, weight_ref[b, c]).astype(BF16) for c in range(3))


def head_masks(width):
    lane = lax.broadcasted_iota(jnp.int32, (1, width), 1)
    return [
        (lane >= h * HEAD_DIM) & (lane < (h + 1) * HEAD_DIM) for h in range(width // HEAD_DIM)
    ]


def pick(mask, value):
    return jnp.where(mask, value, jnp.zeros_like(value))


def head_probs(queries, keys, mask, same):
    scores = dot_nt(pick(mask, queries), keys) * (1.0 / math.sqrt(HEAD_DIM))
    if same is not None:
        scores = jnp.where(same, scores, -jnp.inf)
    shifted = jnp.exp(scores - jnp.max(scores, axis=-1, keepdims=True))
    return shifted / jnp.sum(shifted, axis=-1, keepdims=True)


def same_patch(total, seqs, part):
    row = lax.broadcasted_iota(jnp.int32, (total, total), 0)
    col = lax.broadcasted_iota(jnp.int32, (total, total), 1)
    block = seqs * part
    return (row // block == col // block) & (row % part == col % part)


def backward_heads(queries, keys, values, grad_attn, probs_of):
    masks = head_masks(queries.shape[1])
    grads = [jnp.zeros(queries.shape, F32) for _ in range(3)]
    for h, mask in enumerate(masks):
        probs = probs_of(h, mask)
        grad_probs = dot_nt(pick(mask, grad_attn), values)
        mean = jnp.sum(probs * grad_probs, axis=-1, keepdims=True)
        grad_scores = (probs * (grad_probs - mean) * (1.0 / math.sqrt(HEAD_DIM))).astype(BF16)
        grads[0] = jnp.where(mask, dot_nn(grad_scores, keys), grads[0])
        grads[1] = jnp.where(mask, dot_tn(grad_scores, queries), grads[1])
        grads[2] = jnp.where(mask, dot_tn(probs.astype(BF16), grad_attn), grads[2])
    return [grad.astype(BF16) for grad in grads]


def back_project(grads, weight_ref, b):
    total = dot_nt(grads[0], weight_ref[b, 0])
    total += dot_nt(grads[1], weight_ref[b, 1])
    return total + dot_nt(grads[2], weight_ref[b, 2])


def as_rows(ref):
    return ref[...].astype(F32).reshape(-1, ref.shape[-1])


def put(ref, value):
    ref[...] = value.reshape(ref.shape).astype(BF16)


def spatial_forward(x_ref, shift_ref, scale_ref, weight_ref, out_ref, part_ref, qkv_ref):
    queries, keys, values = project(as_rows(x_ref), shift_ref, scale_ref, weight_ref, 0)
    attended = jnp.zeros(queries.shape, F32)
    for mask in head_masks(queries.shape[1]):
        probs = head_probs(queries, keys, mask, None).astype(BF16)
        attended = jnp.where(mask, dot_nn(probs, values), attended)
    put(part_ref, dot_nn(attended.astype(BF16), out_ref[0]))
    for c, item in enumerate((queries, keys, values)):
        qkv_ref[c] = item


def grad_of_attended(g_ref, gate_ref, out_ref, b):
    grad_proj = (gate_ref[b : b + 1] * as_rows(g_ref)).astype(BF16)
    return dot_nt(grad_proj, out_ref[b]).astype(BF16)


def spatial_backward(g_ref, gate_ref, weight_ref, out_ref, qkv_ref, part_ref):
    queries, keys, values = (qkv_ref[c] for c in range(3))
    grad_attn = grad_of_attended(g_ref, gate_ref, out_ref, 0)
    grads = backward_heads(
        queries, keys, values, grad_attn, lambda h, mask: head_probs(queries, keys, mask, None)
    )
    put(part_ref, back_project(grads, weight_ref, 0))


def temporal(
    x_ref, g_ref, shift_ref, scale_ref, gate_ref, weight_ref, out_ref, part_ref, gpart_ref
):
    _, seqs, part, _ = x_ref.shape
    queries, keys, values = project(as_rows(x_ref), shift_ref, scale_ref, weight_ref, 1)
    same = same_patch(queries.shape[0], seqs, part)
    grad_attn = grad_of_attended(g_ref, gate_ref, out_ref, 1)
    probs = []
    attended = jnp.zeros(queries.shape, F32)
    for mask in head_masks(queries.shape[1]):
        probs.append(head_probs(queries, keys, mask, same))
        attended = jnp.where(mask, dot_nn(probs[-1].astype(BF16), values), attended)
    put(part_ref, dot_nn(attended.astype(BF16), out_ref[1]))
    grads = backward_heads(queries, keys, values, grad_attn, lambda h, mask: probs[h])
    put(gpart_ref, back_project(grads, weight_ref, 1))


def forward_end(total, x_ref, piece, gate_ref, b):
    return (x_ref[piece].astype(F32) + gate_ref[b : b + 1] * total).astype(BF16)


def backward_end(total, x_ref, piece, g_ref, scale_ref, b):
    normed, inv_std = normalize(x_ref[piece])
    grad_norm = total * (1.0 + scale_ref[b : b + 1])
    back = inv_std * (
        grad_norm
        - jnp.mean(grad_norm, axis=-1, keepdims=True)
        - normed * jnp.mean(grad_norm * normed, axis=-1, keepdims=True)
    )
    return (g_ref[piece].astype(F32) + back).astype(BF16)


def head_sums(parts, totals, ends, moved, scratch, seqs, tps, splits):
    inbox, halves, others, sems, seq_sems, own_sem = scratch
    s, z = lax.axis_index("seq"), lax.axis_index("tp")
    chunks = parts[0].shape[0]
    inner = (z > 0) & (z < tps - 1)
    outer = jnp.logical_not(inner)
    near = jnp.where(z < tps // 2, z + 1, z - 1)
    far = jnp.where(z < tps // 2, z - 1, z + 1)
    across = near
    barrier = pltpu.get_barrier_semaphore()

    def greet(tp):
        pl.semaphore_signal(barrier, inc=1, device_id=(s, tp), device_id_type=MESH)

    greet(near)

    @pl.when(inner)
    def _():
        greet(far)

    any_moved = any(item is not None for item in moved)
    if any_moved:

        @pl.loop(1, seqs)
        def _(k):
            pl.semaphore_signal(
                barrier, inc=1, device_id=(lax.rem(s + k, seqs), z), device_id_type=MESH
            )

    peers = seqs - 1 if any_moved else 0

    @pl.when(inner)
    def _():
        pl.semaphore_wait(barrier, 2 + peers)

    @pl.when(outer)
    def _():
        pl.semaphore_wait(barrier, 1 + peers)

    step = seqs // splits
    items = [(i, k) for k in range(chunks * splits) for i in range(len(parts))]

    def piece_of(k):
        return k // splits, pl.ds(k % splits * step, step)

    def remote(src, dst, kind, i, k, tp):
        return pltpu.make_async_remote_copy(
            src_ref=src.at[piece_of(k)],
            dst_ref=dst.at[piece_of(k)],
            send_sem=sems.at[kind, 0, i, k],
            recv_sem=sems.at[kind, 1, i, k],
            device_id=(s, tp),
            device_id_type=MESH,
        )

    def inward(i, c):
        return remote(parts[i], inbox.at[i], 0, i, c, near)

    def cross(i, c):
        return remote(halves.at[i], others.at[i], 1, i, c, across)

    def outward(i, c):
        return remote(totals[i], totals[i], 2, i, c, far)

    def spread(i, k):
        c, first = k // splits, k % splits * step

        @pl.loop(first, first + step)
        def _(to):
            @pl.when(to != s)
            def _():
                pltpu.make_async_remote_copy(
                    src_ref=totals[i].at[c, to],
                    dst_ref=moved[i].at[c, s],
                    send_sem=seq_sems.at[0, c],
                    recv_sem=seq_sems.at[1, c],
                    device_id=(to, z),
                    device_id_type=MESH,
                ).start()

            @pl.when(to == s)
            def _():
                pltpu.make_async_copy(
                    totals[i].at[c, s], moved[i].at[c, s], own_sem.at[c]
                ).start()

    count = len(items)

    @pl.when(outer)
    def _():
        flight, lead = 4, 8
        for at in range(count + lead):
            if at < count:
                if at >= flight:
                    inward(*items[at - flight]).wait_send()
                inward(*items[at]).start()
            if at >= lead:
                i, k = items[at - lead]
                outward(i, k).wait_recv()
                if moved[i] is not None:
                    spread(i, k)
        for item in items[count - flight :]:
            inward(*item).wait_send()

    @pl.when(inner)
    def _():
        def fold(i, k):
            inward(i, k).wait_recv()
            at = (i, *piece_of(k))
            halves[at] = (parts[i][at[1:]].astype(F32) + inbox[at].astype(F32)).astype(BF16)
            cross(i, k).start()

        def finish(i, k):
            cross(i, k).wait_recv()
            at = (i, *piece_of(k))
            total = halves[at].astype(F32) + others[at].astype(F32)
            totals[i][at[1:]] = ends[i](total, at[1:])
            outward(i, k).start()
            if moved[i] is not None:
                spread(i, k)

        lead = 3
        for at in range(count + lead):
            if at < count:
                fold(*items[at])
            if at >= lead:
                finish(*items[at - lead])
        for i, k in items:
            cross(i, k).wait_send()
            outward(i, k).wait_send()

    for i, c in [(i, c) for c in range(chunks) for i in range(len(parts))]:
        if moved[i] is not None:
            pltpu.make_async_copy(totals[i].at[c, s], moved[i].at[c, s], own_sem.at[c]).wait()
            rest = pl.ds(0, seqs - 1)
            both = pltpu.make_async_remote_copy(
                src_ref=totals[i].at[c, rest],
                dst_ref=moved[i].at[c, rest],
                send_sem=seq_sems.at[0, c],
                recv_sem=seq_sems.at[1, c],
                device_id=(lax.rem(s + 1, seqs), z),
                device_id_type=MESH,
            )
            both.wait_send()
            both.wait_recv()


def middle_kernel(seqs, tps, splits, part_ref, x_ref, gate_ref, mid_ref, total, *scratch):
    ends = [lambda value, at: forward_end(value, x_ref, at, gate_ref, 0)]
    head_sums([part_ref], [total], ends, [mid_ref], scratch, seqs, tps, splits)


def temporal_sums(
    seqs, tps, splits, gpart_ref, part_ref, x_ref, g_ref, gate_ref, scale_ref, result_ref, back_ref,
    total, *scratch
):
    ends = [
        lambda value, at: backward_end(value, x_ref, at, g_ref, scale_ref, 1),
        lambda value, at: forward_end(value, x_ref, at, gate_ref, 1),
    ]
    head_sums(
        [gpart_ref, part_ref], [total, result_ref], ends, [back_ref, None],
        scratch, seqs, tps, splits,
    )


def spatial_sums(seqs, tps, splits, gpart_ref, x_ref, g_ref, scale_ref, grad_ref, *scratch):
    ends = [lambda value, at: backward_end(value, x_ref, at, g_ref, scale_ref, 0)]
    head_sums([gpart_ref], [grad_ref], ends, [None], scratch, seqs, tps, splits)


def compute(body, outs, *operands):
    return pl.pallas_call(
        body,
        out_shape=outs,
        in_specs=[VMEM] * len(operands),
        out_specs=jax.tree.map(lambda _: VMEM, outs),
        compiler_params=pltpu.CompilerParams(vmem_limit_bytes=LIMIT),
    )(*operands)


def exchange(body, ident, outs, streams, own_total, seqs, tps, splits, *operands):
    shape = operands[0].shape
    chunks = shape[0]
    splits = math.gcd(seqs, splits)
    scratch = [pltpu.VMEM(shape, BF16)] if own_total else []
    scratch += [pltpu.VMEM((streams, *shape), BF16)] * 3
    scratch += [
        pltpu.SemaphoreType.DMA((3, 2, streams, chunks * splits)),
        pltpu.SemaphoreType.DMA((2, chunks)),
        pltpu.SemaphoreType.DMA((chunks,)),
    ]
    return pl.pallas_call(
        functools.partial(body, seqs, tps, splits),
        out_shape=outs,
        in_specs=[VMEM] * len(operands),
        out_specs=jax.tree.map(lambda _: VMEM, outs),
        scratch_shapes=scratch,
        compiler_params=pltpu.CompilerParams(
            collective_id=ident, has_side_effects=True, vmem_limit_bytes=LIMIT
        ),
    )(*operands)


def per_device(
    seqs, tps, tokens, grad_out, qkv_weight, out_weight, mod_shift, mod_scale, mod_gate
):
    width = tokens.shape[-1]
    patches = tokens.shape[0] // seqs
    chunks = max(1, patches // 8)
    part = patches // chunks
    dims = (chunks, seqs, part, width)
    array = jax.ShapeDtypeStruct(dims, BF16)
    weights = jnp.transpose(qkv_weight, (0, 2, 1, 3))
    x = tokens.reshape(seqs, chunks, part, width).transpose(1, 0, 2, 3)
    g = grad_out.reshape(chunks, part, seqs, width).transpose(0, 2, 1, 3)

    cached = jax.ShapeDtypeStruct((3, tokens.shape[0], out_weight.shape[1]), BF16)
    part_s, qkv_s = compute(
        spatial_forward, (array, cached), x, mod_shift, mod_scale, weights, out_weight
    )
    mid = exchange(middle_kernel, 0, array, 1, True, seqs, tps, 4, part_s, x, mod_gate)
    part_t, gpart_t = compute(
        temporal, (array, array),
        mid, g, mod_shift, mod_scale, mod_gate, weights, out_weight,
    )
    result, grad_mid = exchange(
        temporal_sums, 1, (array, array), 2, True, seqs, tps, 2,
        gpart_t, part_t, mid, g, mod_gate, mod_scale,
    )
    gpart_s = compute(spatial_backward, array, grad_mid, mod_gate, weights, out_weight, qkv_s)
    grad_in = exchange(
        spatial_sums, 2, array, 1, False, seqs, tps, 4, gpart_s, x, grad_mid, mod_scale
    )
    result = result.transpose(0, 2, 1, 3).reshape(grad_out.shape)
    return (result, grad_in.transpose(1, 0, 2, 3).reshape(tokens.shape))


def solution(mesh):
    in_specs = (
        P(None, "seq", None),
        P("seq", None, None),
        P(None, None, None, "tp"),
        P(None, "tp", None),
        P(),
        P(),
        P(),
    )
    out_specs = (P("seq", None, None), P(None, "seq", None))
    return jax.shard_map(
        functools.partial(per_device, mesh.shape["seq"], mesh.shape["tp"]),
        mesh=mesh,
        in_specs=in_specs,
        out_specs=out_specs,
        check_vma=False,
    )
```

time: 130 us -> 134 us (1.031)
  Pallas kernels: 115 us -> 122 us
  local copies, waits for them, and re-layouts: 13.5 us -> 10.7 us
    pallas_call x3, Pallas kernels: 14.1 us -> 21.6 us  [compute(): pl.pallas_call(body, out_shape=outs, in_specs=[VMEM] * len(operands), out...]
    squeeze x2 -> x0, local copies, waits for them, and re-layouts: 3.29 us -> none  [the longest x1 3.18 us: per_device(): weights[1]]
where the time goes in v2:
time: 134 us
  Pallas kernels  122 us (91%)
  local copies, waits for them, and re-layouts  10.7 us (8%)
    pallas_call x3, Pallas kernels, exchange(): pl.pallas_call(functools.partial(body, seqs, tps, splits), out_shape=outs...  101 us
    pallas_call x3, Pallas kernels, compute(): pl.pallas_call(body, out_shape=outs, in_specs=[VMEM] * len(operands), out...  21.6 us
    unnamed x9, local copies, waits for them, and re-layouts  6.68 us

profile of v2, /device:TPU:0, one launch (start us, length us, event | category | flops | bytes accessed | tf_op | source)
XLA Modules:
  0.0 133.5 jit_solution(11747341691128886530)
XLA Ops:
  0.6 1.1 copy.18
  1.7 1.1 copy.17
  2.9 0.0 copy-start
  2.9 0.0 copy-start.2
  2.9 0.0 copy-start.3
  2.9 6.7 %copy.11 = bf16[2,1152,3,288]{3,1,2,0:T(8,128)(2,1)} copy(bf16[2,1152,3,288]{1,3,2,0:T(8,128)(2,1)} %param.9) | data formatting | bytes 7962624 | tf_op args[2]
  9.6 0.0 copy-start.1
  9.6 0.0 copy-done
  9.6 0.0 copy-done.2
  9.6 0.0 copy-done.3
  9.6 5.7 %shard_map.86 = (bf16[4,8,8,1152]{3,2,1,0:T(8,128)(2,1)S(1)}, bf16[3,256,288]{2,1,0:T(8,128)(2,1)S(1)}) custom-call(bf16[4,8,8,1152]{3,2,1,0:T(8,128)(2,1)S(1)} %bitcast.13, f32[2,1152]{1,0:T(2,128)S(1)} %copy-done.3, f32[2,1152]{1,0:T(2,128)S(1)} %copy-done.2, bf16[2,3,1152,288]{3,2,1,0:T(8,128)(2,1)} %bitcast.20, bf16[2,288,1152]{2,1,0:T(8,128)(2,1)S(1)} %copy-done), custom_call_target="tpu_custom_call" | custom-call | tf_op jit(solution)/shard_map/pallas_call | solution.py:327
  15.3 0.0 copy-done.1
  15.3 32.2 %shard_map.87.x_ref = bf16[4,8,8,1152]{3,2,1,0:T(8,128)(2,1)S(1)} custom-call(bf16[4,8,8,1152]{3,2,1,0:T(8,128)(2,1)S(1)} %get-tuple-element.8.part_ref, bf16[4,8,8,1152]{3,2,1,0:T(8,128)(2,1)S(1)} %bitcast.14, f32[2,1152]{1,0:T(2,128)S(1)} %copy-done.1), custom_call_target="tpu_custom_call" | custom-call | tf_op jit(solution)/shard_map/pallas_call | solution.py:347
  47.6 8.8 %shard_map.88 = (bf16[4,8,8,1152]{3,2,1,0:T(8,128)(2,1)S(1)}, bf16[4,8,8,1152]{3,2,1,0:T(8,128)(2,1)S(1)}) custom-call(bf16[4,8,8,1152]{3,2,1,0:T(8,128)(2,1)S(1)} %shard_map.87.x_ref, bf16[4,8,8,1152]{3,2,1,0:T(8,128)(2,1)S(1)} %bitcast.16, f32[2,1152]{1,0:T(2,128)S(1)} %copy-done.3, f32[2,1152]{1,0:T(2,128)S(1)} %copy-done.2, f32[2,1152]{1,0:T(2,128)S(1)} %copy-done.1, ...), custom_call_target="tpu_custom_call" | custom-call | tf_op jit(solution)/shard_map/pallas_call | solution.py:327
  56.4 41.1 %shard_map.89 = (bf16[4,8,8,1152]{3,2,1,0:T(8,128)(2,1)S(1)}, bf16[4,8,8,1152]{3,2,1,0:T(8,128)(2,1)S(1)}) custom-call(bf16[4,8,8,1152]{3,2,1,0:T(8,128)(2,1)S(1)} %get-tuple-element.9.gpart_ref, bf16[4,8,8,1152]{3,2,1,0:T(8,128)(2,1)S(1)} %get-tuple-element.10.part_ref, bf16[4,8,8,1152]{3,2,1,0:T(8,128)(2,1)S(1)} %shard_map.87.x_ref, ...), custom_call_target="tpu_custom_call" | custom-call | tf_op jit(solution)/shard_map/pallas_call | solution.py:347
  97.6 7.0 %shard_map.90.gpart_ref = bf16[4,8,8,1152]{3,2,1,0:T(8,128)(2,1)S(1)} custom-call(bf16[4,8,8,1152]{3,2,1,0:T(8,128)(2,1)S(1)} %get-tuple-element.12.g_ref, f32[2,1152]{1,0:T(2,128)S(1)} %copy-done.1, bf16[2,3,1152,288]{3,2,1,0:T(8,128)(2,1)} %bitcast.22, bf16[2,288,1152]{2,1,0:T(8,128)(2,1)S(1)} %copy-done, bf16[3,256,288]{2,1,0:T(8,128)(2,1)S(1)} %get-tuple-element.13.qkv_ref), custom_call_target="tpu_custom_call" | custom-call | tf_op jit(solution)/shard_map/pallas_call | solution.py:327
  104.6 27.2 %shard_map.91 = bf16[4,8,8,1152]{3,2,1,0:T(8,128)(2,1)S(1)} custom-call(bf16[4,8,8,1152]{3,2,1,0:T(8,128)(2,1)S(1)} %shard_map.90.gpart_ref, bf16[4,8,8,1152]{3,2,1,0:T(8,128)(2,1)S(1)} %bitcast.15, bf16[4,8,8,1152]{3,2,1,0:T(8,128)(2,1)S(1)} %get-tuple-element.12.g_ref, f32[2,1152]{1,0:T(2,128)S(1)} %copy-done.2), custom_call_target="tpu_custom_call" | custom-call | tf_op jit(solution)/shard_map/pallas_call | solution.py:347
  131.8 0.9 copy.13
  132.7 0.9 copy.14
Async XLA Ops:
  2.9 6.7 %copy-start = (bf16[2,288,1152]{2,1,0:T(8,128)(2,1)S(1)}, bf16[2,288,1152]{2,1,0:T(8,128)(2,1)}, u32[]{:S(2)}) copy-start(bf16[2,288,1152]{2,1,0:T(8,128)(2,1)} %out_ref.5) | copy-start | bytes 3981316
  2.9 6.7 %copy-start.2 = (f32[2,1152]{1,0:T(2,128)S(1)}, f32[2,1152]{1,0:T(2,128)}, u32[]{:S(2)}) copy-start(f32[2,1152]{1,0:T(2,128)} %scale_ref.7) | copy-start | bytes 27652
  2.9 6.7 %copy-start.3 = (f32[2,1152]{1,0:T(2,128)S(1)}, f32[2,1152]{1,0:T(2,128)}, u32[]{:S(2)}) copy-start(f32[2,1152]{1,0:T(2,128)} %shift_ref.3) | copy-start | bytes 27652
  9.6 5.8 %copy-start.1 = (f32[2,1152]{1,0:T(2,128)S(1)}, f32[2,1152]{1,0:T(2,128)}, u32[]{:S(2)}) copy-start(f32[2,1152]{1,0:T(2,128)} %gate_ref.7) | copy-start | bytes 27652

commit v3 on v2

--- a/solution.py
+++ b/solution.py
@@ -13,7 +13,7 @@
 F32 = jnp.float32
 MESH = pl.DeviceIdType.MESH
 VMEM = pl.BlockSpec(memory_space=pltpu.VMEM)
-LIMIT = 48 * 1024 * 1024
+LIMIT = 28 * 1024 * 1024
 
 
 def dot_nn(a, b):
@@ -242,7 +242,7 @@
 
     @pl.when(outer)
     def _():
-        flight, lead = 4, 8
+        flight, lead = 4, 6
         for at in range(count + lead):
             if at < count:
                 if at >= flight:
@@ -373,7 +373,7 @@
     part_s, qkv_s = compute(
         spatial_forward, (array, cached), x, mod_shift, mod_scale, weights, out_weight
     )
-    mid = exchange(middle_kernel, 0, array, 1, True, seqs, tps, 4, part_s, x, mod_gate)
+    mid = exchange(middle_kernel, 0, array, 1, True, seqs, tps, 2, part_s, x, mod_gate)
     part_t, gpart_t = compute(
         temporal, (array, array),
         mid, g, mod_shift, mod_scale, mod_gate, weights, out_weight,
@@ -384,7 +384,7 @@
     )
     gpart_s = compute(spatial_backward, array, grad_mid, mod_gate, weights, out_weight, qkv_s)
     grad_in = exchange(
-        spatial_sums, 2, array, 1, False, seqs, tps, 4, gpart_s, x, grad_mid, mod_scale
+        spatial_sums, 2, array, 1, False, seqs, tps, 2, gpart_s, x, grad_mid, mod_scale
     )
     result = result.transpose(0, 2, 1, 3).reshape(grad_out.shape)
     return (result, grad_in.transpose(1, 0, 2, 3).reshape(tokens.shape))

time: 134 us -> 126 us (0.940)
  Pallas kernels: 122 us -> 112 us
  local copies, waits for them, and re-layouts: 10.7 us -> 13.2 us
    pallas_call x3, Pallas kernels: 21.6 us -> 14.1 us  [compute(): pl.pallas_call(body, out_shape=outs, in_specs=[VMEM] * len(operands), out...]
    pallas_call x3, Pallas kernels: 101 us -> 97.8 us  [exchange(): pl.pallas_call(functools.partial(body, seqs, tps, splits), out_shape=outs...]
    unnamed x9 -> x13, local copies, waits for them, and re-layouts: 6.68 us -> 9.18 us
where the time goes in v3:
time: 126 us
  Pallas kernels  112 us (89%)
  local copies, waits for them, and re-layouts  13.2 us (10%)
    pallas_call x3, Pallas kernels, exchange(): pl.pallas_call(functools.partial(body, seqs, tps, splits), out_shape=outs...  97.8 us
    pallas_call x3, Pallas kernels, compute(): pl.pallas_call(body, out_shape=outs, in_specs=[VMEM] * len(operands), out...  14.1 us
    unnamed x13, local copies, waits for them, and re-layouts  9.18 us

profile of v3, /device:TPU:0, one launch (start us, length us, event | category | flops | bytes accessed | tf_op | source)
XLA Modules:
  0.0 125.8 jit_solution(6404265899600956210)
XLA Ops:
  0.6 1.1 copy.18
  1.7 1.1 copy.17
  2.9 0.0 copy-start.2
  2.9 0.0 copy-start.4
  2.9 0.0 copy-start.5
  2.9 6.7 %copy.11 = bf16[2,1152,3,288]{3,1,2,0:T(8,128)(2,1)} copy(bf16[2,1152,3,288]{1,3,2,0:T(8,128)(2,1)} %param.9) | data formatting | bytes 7962624 | tf_op args[2]
  9.6 0.0 copy-done.2
  9.6 0.0 copy-done.4
  9.6 0.0 copy-done.5
  9.6 0.0 copy-start
  9.6 2.5 %copy-done = bf16[2,1152,3,288]{3,1,2,0:T(8,128)(2,1)S(1)} copy-done((bf16[2,1152,3,288]{3,1,2,0:T(8,128)(2,1)S(1)}, bf16[2,1152,3,288]{3,1,2,0:T(8,128)(2,1)}, u32[]{:S(2)}) %copy-start) | copy-done | bytes 3981336
  12.1 0.0 copy-start.3
  12.1 0.0 copy-start.1
  12.1 3.3 %shard_map.86 = (bf16[4,8,8,1152]{3,2,1,0:T(8,128)(2,1)S(1)}, bf16[3,256,288]{2,1,0:T(8,128)(2,1)S(1)}) custom-call(bf16[4,8,8,1152]{3,2,1,0:T(8,128)(2,1)S(1)} %bitcast.16, f32[2,1152]{1,0:T(2,128)S(1)} %copy-done.5, f32[2,1152]{1,0:T(2,128)S(1)} %copy-done.4, bf16[2,3,1152,288]{3,2,1,0:T(8,128)(2,1)S(1)} %bitcast.13, bf16[2,288,1152]{2,1,0:T(8,128)(2,1)S(1)} %copy-done.2), custom_call_target="tpu_custom_call" | custom-call | tf_op jit(solution)/shard_map/pallas_call | solution.py:327
  15.4 0.0 copy-done.3
  15.4 31.1 %shard_map.87.x_ref = bf16[4,8,8,1152]{3,2,1,0:T(8,128)(2,1)S(1)} custom-call(bf16[4,8,8,1152]{3,2,1,0:T(8,128)(2,1)S(1)} %get-tuple-element.8.part_ref, bf16[4,8,8,1152]{3,2,1,0:T(8,128)(2,1)S(1)} %bitcast.17, f32[2,1152]{1,0:T(2,128)S(1)} %copy-done.3), custom_call_target="tpu_custom_call" | custom-call | tf_op jit(solution)/shard_map/pallas_call | solution.py:347
  46.5 0.0 copy-done.1
  46.5 6.3 %shard_map.88 = (bf16[4,8,8,1152]{3,2,1,0:T(8,128)(2,1)S(1)}, bf16[4,8,8,1152]{3,2,1,0:T(8,128)(2,1)S(1)}) custom-call(bf16[4,8,8,1152]{3,2,1,0:T(8,128)(2,1)S(1)} %shard_map.87.x_ref, bf16[4,8,8,1152]{3,2,1,0:T(8,128)(2,1)S(1)} %bitcast.19, f32[2,1152]{1,0:T(2,128)S(1)} %copy-done.5, f32[2,1152]{1,0:T(2,128)S(1)} %copy-done.4, f32[2,1152]{1,0:T(2,128)S(1)} %copy-done.3, ...), custom_call_target="tpu_custom_call" | custom-call | tf_op jit(solution)/shard_map/pallas_call | solution.py:327
  52.8 43.0 %shard_map.89 = (bf16[4,8,8,1152]{3,2,1,0:T(8,128)(2,1)S(1)}, bf16[4,8,8,1152]{3,2,1,0:T(8,128)(2,1)S(1)}) custom-call(bf16[4,8,8,1152]{3,2,1,0:T(8,128)(2,1)S(1)} %get-tuple-element.9.gpart_ref, bf16[4,8,8,1152]{3,2,1,0:T(8,128)(2,1)S(1)} %get-tuple-element.10.part_ref, bf16[4,8,8,1152]{3,2,1,0:T(8,128)(2,1)S(1)} %shard_map.87.x_ref, ...), custom_call_target="tpu_custom_call" | custom-call | tf_op jit(solution)/shard_map/pallas_call | solution.py:347
  95.8 4.5 %shard_map.90.gpart_ref = bf16[4,8,8,1152]{3,2,1,0:T(8,128)(2,1)S(1)} custom-call(bf16[4,8,8,1152]{3,2,1,0:T(8,128)(2,1)S(1)} %get-tuple-element.12.g_ref, f32[2,1152]{1,0:T(2,128)S(1)} %copy-done.3, bf16[2,3,1152,288]{3,2,1,0:T(8,128)(2,1)S(1)} %bitcast.15, bf16[2,288,1152]{2,1,0:T(8,128)(2,1)S(1)} %copy-done.2, ...), custom_call_target="tpu_custom_call" | custom-call | tf_op jit(solution)/shard_map/pallas_call | solution.py:327
  100.3 23.7 %shard_map.91 = bf16[4,8,8,1152]{3,2,1,0:T(8,128)(2,1)S(1)} custom-call(bf16[4,8,8,1152]{3,2,1,0:T(8,128)(2,1)S(1)} %shard_map.90.gpart_ref, bf16[4,8,8,1152]{3,2,1,0:T(8,128)(2,1)S(1)} %bitcast.18, bf16[4,8,8,1152]{3,2,1,0:T(8,128)(2,1)S(1)} %get-tuple-element.12.g_ref, f32[2,1152]{1,0:T(2,128)S(1)} %copy-done.4), custom_call_target="tpu_custom_call" | custom-call | tf_op jit(solution)/shard_map/pallas_call | solution.py:347
  124.0 0.9 copy.13
  124.9 0.9 copy.14
Async XLA Ops:
  2.9 6.7 %copy-start.2 = (bf16[2,288,1152]{2,1,0:T(8,128)(2,1)S(1)}, bf16[2,288,1152]{2,1,0:T(8,128)(2,1)}, u32[]{:S(2)}) copy-start(bf16[2,288,1152]{2,1,0:T(8,128)(2,1)} %out_ref.5) | copy-start | bytes 3981316
  2.9 6.7 %copy-start.4 = (f32[2,1152]{1,0:T(2,128)S(1)}, f32[2,1152]{1,0:T(2,128)}, u32[]{:S(2)}) copy-start(f32[2,1152]{1,0:T(2,128)} %scale_ref.7) | copy-start | bytes 27652
  2.9 6.7 %copy-start.5 = (f32[2,1152]{1,0:T(2,128)S(1)}, f32[2,1152]{1,0:T(2,128)}, u32[]{:S(2)}) copy-start(f32[2,1152]{1,0:T(2,128)} %shift_ref.3) | copy-start | bytes 27652
  9.6 2.5 %copy-start = (bf16[2,1152,3,288]{3,1,2,0:T(8,128)(2,1)S(1)}, bf16[2,1152,3,288]{3,1,2,0:T(8,128)(2,1)}, u32[]{:S(2)}) copy-start(bf16[2,1152,3,288]{3,1,2,0:T(8,128)(2,1)} %copy.11) | copy-start | bytes 11943940
  12.1 3.3 %copy-start.3 = (f32[2,1152]{1,0:T(2,128)S(1)}, f32[2,1152]{1,0:T(2,128)}, u32[]{:S(2)}) copy-start(f32[2,1152]{1,0:T(2,128)} %gate_ref.7) | copy-start | bytes 27652
  12.1 34.4 %copy-start.1 = (bf16[2,1152,3,288]{3,1,2,0:T(8,128)(2,1)S(1)}, bf16[2,1152,3,288]{3,1,2,0:T(8,128)(2,1)}, u32[]{:S(2)}) copy-start(bf16[2,1152,3,288]{3,1,2,0:T(8,128)(2,1)} %copy.11) | copy-start | bytes 11943940
